TPU v7x, 32 devices: a whole 2x2x4 slice. The times are simulated.
32 devices in a mesh: dp: 4 (over y, core), expert: 8 (over z, x).
Axes of the slice: x: 2, y: 2, z: 4, core: 2. Of those that a mesh axis runs over, the one named last changes fastest.
Arguments:
- tokens: bfloat16 [8192, 4096], P(('dp', 'expert')), may hold values from -6 to 6
- routes: int32 [8192, 2], P(('dp', 'expert')), may hold values from 0 to 7, all different within a row; in each aligned block of 256 rows (0 to 255, 256 to 511, ...) at most 128 rows name the same one
- route_weights: float32 [8192, 2], P(('dp', 'expert')), may hold values from 0.1 to 0.9
- placement: int32 [8], replicated, may hold values from 0 to 7, each once
- expert_weights: bfloat16 [8, 4096, 1024], P('expert', None, 'dp'), may hold values from -0.09375 to 0.09375
- grads: bfloat16 [8, 4096, 1024], P('expert', None, 'dp'), may hold values from -0.059814453 to 0.059814453
- first_moment: bfloat16 [8, 4096, 1024], P('expert', None, 'dp'), may hold values from -0.017944336 to 0.017944336
- second_moment: bfloat16 [8, 4096, 1024], P('expert', None, 'dp'), may hold values from 9.953976e-06 to 0.0009994507
Outputs:
- new_weights: bfloat16 [8, 4096, 1024], P('expert', None, 'dp')
- new_first: bfloat16 [8, 4096, 1024], P('expert', None, 'dp')
- new_second: bfloat16 [8, 4096, 1024], P('expert', None, 'dp')
- mixed: bfloat16 [8192, 1024], P(('dp', 'expert'))
Inputs may be any that keep to these rules, and one draw needn't show every extreme that they name: `routes`: each token names two different experts; within the rows of one device no expert is named more than 128 times, a bound that some block reaches. `placement`: each expert appears exactly once.
All inputs are finite; a program needn't handle non-finite values.
Results may differ from a plain program's by a relative error of at most 0.0057.
Values may be sent and summed in bfloat16 or wider, within the bound.
No kernel may reach another device: no remote copies, remote signals or barrier semaphores. Data moves between devices by JAX's collectives and lax.ppermute only.
A program may use at most 192 MiB of HBM per device.

v0:
```python
import jax
import jax.numpy as jnp
from jax import lax
from jax.sharding import PartitionSpec as P

beta_one = 0.9
beta_two = 0.999
learn_rate = 0.008
adam_eps = 1e-08


def adam_step(weight, gradient, first, second):
    grad_wide = gradient.astype(jnp.float32)
    first_wide = beta_one * first.astype(jnp.float32) + (1.0 - beta_one) * grad_wide
    second_wide = beta_two * second.astype(jnp.float32) + (1.0 - beta_two) * grad_wide * grad_wide
    updated = weight.astype(jnp.float32) - learn_rate * first_wide / (
        jnp.sqrt(second_wide) + adam_eps
    )
    return (
        updated.astype(jnp.bfloat16),
        first_wide.astype(jnp.bfloat16),
        second_wide.astype(jnp.bfloat16),
    )


def to_pieces(slab, count):
    return slab.reshape(count, slab.shape[0] // count, slab.shape[1])


def from_pieces(pieces):
    return pieces.reshape(pieces.shape[0] * pieces.shape[1], pieces.shape[2])


def shards(
    tokens, routes, route_weights, placement, expert_weights, grads, first_moment, second_moment
):
    experts = lax.axis_size("expert")
    width = tokens.shape[1]
    spread = (
        lax.all_to_all(
            to_pieces(expert_weights[0], experts), "expert", split_axis=0, concat_axis=0, tiled=True
        ),
        lax.all_to_all(
            to_pieces(grads[0], experts), "expert", split_axis=0, concat_axis=0, tiled=True
        ),
        lax.all_to_all(
            to_pieces(first_moment[0], experts), "expert", split_axis=0, concat_axis=0, tiled=True
        ),
        lax.all_to_all(
            to_pieces(second_moment[0], experts), "expert", split_axis=0, concat_axis=0, tiled=True
        ),
    )
    chosen = tuple((jnp.take(member, placement, axis=0) for member in spread))
    collected = (
        lax.all_to_all(chosen[0], "expert", split_axis=0, concat_axis=0, tiled=True),
        lax.all_to_all(chosen[1], "expert", split_axis=0, concat_axis=0, tiled=True),
        lax.all_to_all(chosen[2], "expert", split_axis=0, concat_axis=0, tiled=True),
        lax.all_to_all(chosen[3], "expert", split_axis=0, concat_axis=0, tiled=True),
    )
    new_slab, first_slab, second_slab = adam_step(
        from_pieces(collected[0]),
        from_pieces(collected[1]),
        from_pieces(collected[2]),
        from_pieces(collected[3]),
    )
    tok_count = tokens.shape[0]
    capacity = 4 * tok_count // experts
    expert_ids = jnp.arange(experts, dtype=jnp.int32)
    entries = routes.reshape(2 * tok_count)
    onehot = (entries[:, None] == expert_ids[None, :]).astype(jnp.int32)
    before = jnp.cumsum(onehot, axis=0) - onehot
    position = jnp.sum(before * onehot, axis=1)
    hosting = jnp.sum(
        jnp.where(placement[None, :] == expert_ids[:, None], expert_ids[None, :], 0), axis=1
    )
    target_dev = jnp.sum(onehot * hosting[None, :], axis=1)
    target_slot = target_dev * capacity + position
    select = (
        target_slot[:, None] == jnp.arange(experts * capacity, dtype=jnp.int32)[None, :]
    ).astype(jnp.bfloat16)
    select_pairs = select.reshape(tok_count, 2, experts * capacity)
    select_tokens = jnp.sum(select_pairs, axis=1)
    outgoing = jnp.einsum(
        "ts,td->sd", select_tokens, tokens, preferred_element_type=jnp.float32
    ).astype(jnp.bfloat16)
    received = lax.all_to_all(
        outgoing.reshape(experts, capacity, width),
        "expert",
        split_axis=0,
        concat_axis=0,
        tiled=True,
    )
    slot_rows = received.reshape(experts * capacity, width)
    acts = jax.nn.silu(
        jnp.dot(
            slot_rows,
            lax.all_gather(new_slab, "dp", axis=1, tiled=True),
            preferred_element_type=jnp.float32,
        )
    ).astype(jnp.bfloat16)
    hidden = acts.shape[1]
    returned = lax.all_to_all(
        acts.reshape(experts, capacity, hidden), "expert", split_axis=0, concat_axis=0, tiled=True
    )
    back_rows = returned.reshape(experts * capacity, hidden)
    picked = jnp.einsum("tks,sh->tkh", select_pairs, back_rows, preferred_element_type=jnp.float32)
    mixed = jnp.sum(route_weights[:, :, None] * picked, axis=1).astype(jnp.bfloat16)
    return (new_slab[None], first_slab[None], second_slab[None], mixed)


def solution(mesh):
    return jax.shard_map(
        shards,
        mesh=mesh,
        in_specs=(
            P(("dp", "expert"), None),
            P(("dp", "expert"), None),
            P(("dp", "expert"), None),
            P(),
            P("expert", None, "dp"),
            P("expert", None, "dp"),
            P("expert", None, "dp"),
            P("expert", None, "dp"),
        ),
        out_specs=(
            P("expert", None, "dp"),
            P("expert", None, "dp"),
            P("expert", None, "dp"),
            P(("dp", "expert"), None),
        ),
        check_vma=False,
    )
```

profile of v0, /device:TPU:0, one launch (start us, length us, event | category | flops | bytes accessed | tf_op | source)
XLA Modules:
  0.0 698.4 jit_solution(7767158036233627692)
XLA Ops:
  7.2 0.0 copy-start
  7.2 55.9 %all_to_all.50 = bf16[8,512,256]{2,1,0:T(8,128)(2,1)} all-to-all(bf16[8,512,256]{2,1,0:T(8,128)(2,1)} %bitcast.87), channel_id=1, replica_groups=mesh['dp'=4,'expert'=8] {'expert'}, dimensions={0} | all-to-all | bytes 4194304 | tf_op jit(solution)/shard_map/all_to_all | solution.py:40
  63.1 51.6 %all_to_all.51 = bf16[8,512,256]{2,1,0:T(8,128)(2,1)} all-to-all(bf16[8,512,256]{2,1,0:T(8,128)(2,1)S(1)} %bitcast.88), channel_id=1, replica_groups=mesh['dp'=4,'expert'=8] {'expert'}, dimensions={0} | all-to-all | bytes 4194304 | tf_op jit(solution)/shard_map/all_to_all | solution.py:43
  114.7 51.2 %all_to_all.52 = bf16[8,512,256]{2,1,0:T(8,128)(2,1)} all-to-all(bf16[8,512,256]{2,1,0:T(8,128)(2,1)S(1)} %bitcast.89), channel_id=1, replica_groups=mesh['dp'=4,'expert'=8] {'expert'}, dimensions={0} | all-to-all | bytes 4194304 | tf_op jit(solution)/shard_map/all_to_all | solution.py:46
  165.9 4.5 all-to-all-start.6
  170.4 0.0 copy-done.13
  170.4 3.6 gather_fusion
  174.0 3.6 gather_fusion.2
  177.6 3.6 gather_fusion.1
  181.2 36.4 %all-to-all-done.6 = bf16[8,512,256]{2,1,0:T(8,128)(2,1)} async-done(((bf16[8,512,256]{2,1,0:T(8,128)(2,1)}), bf16[8,512,256]{2,1,0:T(8,128)(2,1)}, u32[]{:S(2)}, u32[]{:S(2)}) %all-to-all-start.6) | async-done | bytes 2097184 | tf_op jit(solution)/shard_map/all_to_all | solution.py:49
  217.6 3.6 gather_fusion.3
  221.2 5.6 broadcast_select_fusion
  226.8 51.9 %all_to_all.53 = bf16[8,512,256]{2,1,0:T(8,128)(2,1)} all-to-all(bf16[8,512,256]{2,1,0:T(8,128)(2,1)S(1)} %get-tuple-element.10), channel_id=1, replica_groups=mesh['dp'=4,'expert'=8] {'expert'}, dimensions={0} | all-to-all | bytes 4194304 | tf_op jit(solution)/shard_map/all_to_all | solution.py:58
  278.6 51.5 %all_to_all.54 = bf16[8,512,256]{2,1,0:T(8,128)(2,1)} all-to-all(bf16[8,512,256]{2,1,0:T(8,128)(2,1)S(1)} %get-tuple-element.11), channel_id=1, replica_groups=mesh['dp'=4,'expert'=8] {'expert'}, dimensions={0} | all-to-all | bytes 4194304 | tf_op jit(solution)/shard_map/all_to_all | solution.py:57
  330.1 51.2 %all_to_all.55 = bf16[8,512,256]{2,1,0:T(8,128)(2,1)} all-to-all(bf16[8,512,256]{2,1,0:T(8,128)(2,1)S(1)} %get-tuple-element.12), channel_id=1, replica_groups=mesh['dp'=4,'expert'=8] {'expert'}, dimensions={0} | all-to-all | bytes 4194304 | tf_op jit(solution)/shard_map/all_to_all | solution.py:56
  381.4 4.5 all-to-all-start.1
  385.9 0.0 copy-done.11
  385.9 0.1 copy.16
  386.0 0.1 eq.81
  386.2 0.1 eq.74
  386.3 1.1 reduce-window.6
  387.5 0.2 slice_reduce_fusion
  387.7 0.1 select_reduce_fusion.1
  387.8 0.1 select_reduce_fusion
  388.0 0.1 add.71
  388.1 0.1 copy.18
  388.2 0.3 fusion.19
  388.5 5.6 convolution_convert_fusion
  394.1 39.0 %all-to-all-done.1 = bf16[8,512,256]{2,1,0:T(8,128)(2,1)} async-done(((bf16[8,512,256]{2,1,0:T(8,128)(2,1)}), bf16[8,512,256]{2,1,0:T(8,128)(2,1)}, u32[]{:S(2)}, u32[]{:S(2)}) %all-to-all-start.1) | async-done | bytes 2097184 | tf_op jit(solution)/shard_map/all_to_all | solution.py:55
  433.1 5.1 all-to-all-start.8
  438.2 0.2 all-gather.2.cloned.1.call-start
  438.4 0.4 convert_multiply_fusion.1
  438.8 1.2 copy-done.7
  440.0 0.4 convert_multiply_fusion
  440.4 1.7 copy-done.2
  442.1 1.9 copy-done.4
  444.1 6.1 fusion.10
  450.2 0.0 all-gather.2.cloned.1.call-update
  450.2 170.0 %all-to-all-done.8 = bf16[8,128,4096]{2,1,0:T(8,128)(2,1)} async-done(((bf16[8,128,4096]{2,1,0:T(8,128)(2,1)}), bf16[8,128,4096]{2,1,0:T(8,128)(2,1)}, u32[]{:S(2)}, u32[]{:S(2)}) %all-to-all-start.8) | async-done | bytes 8388640 | tf_op jit(solution)/shard_map/all_to_all | solution.py:86
  620.2 15.3 %multiply_convert_fusion = bf16[1024,1024]{1,0:T(8,128)(2,1)} fusion(bf16[1024,4096]{1,0:T(8,128)(2,1)} %bitcast.12, bf16[4096,1024]{1,0:T(8,128)(2,1)} %all-gather.2.cloned.1.call-done), kind=kOutput, calls=%fused_computation.20 | convolution fusion | flops 8595177472 | bytes 18874368 | tf_op jit(solution)/shard_map/dot_general | solution.py:95
  635.5 4.3 all-to-all-start.9
  639.8 2.1 convert_element_type.150
  642.0 0.4 convert_element_type.151
  642.3 0.3 copy-done.5
  642.6 1.7 copy-done.3
  644.3 4.5 fusion.16
  648.8 38.8 %all-to-all-done.9 = bf16[8,128,1024]{2,1,0:T(8,128)(2,1)} async-done(((bf16[8,128,1024]{2,1,0:T(8,128)(2,1)}), bf16[8,128,1024]{2,1,0:T(8,128)(2,1)}, u32[]{:S(2)}, u32[]{:S(2)}) %all-to-all-start.9) | async-done | bytes 2097184 | tf_op jit(solution)/shard_map/all_to_all | solution.py:102
  687.6 4.0 multiply_reduce_fusion
  (28 shorter events, 0.1 us)
Async XLA Ops:
  7.2 381.3 %copy-start = (bf16[256,4096]{1,0:T(8,128)(2,1)S(1)}, bf16[256,4096]{1,0:T(8,128)(2,1)}, u32[]{:S(2)}) copy-start(bf16[256,4096]{1,0:T(8,128)(2,1)} %param.10) | copy-start | bytes 6291460
  7.2 55.9 %copy-start.9 = (bf16[1,4096,256]{2,1,0:T(8,128)(2,1)S(1)}, bf16[1,4096,256]{2,1,0:T(8,128)(2,1)}, u32[]{:S(2)}) copy-start(bf16[1,4096,256]{2,1,0:T(8,128)(2,1)} %param.15) | copy-start | bytes 6291460
  63.1 51.6 %copy-start.10 = (bf16[1,4096,256]{2,1,0:T(8,128)(2,1)S(1)}, bf16[1,4096,256]{2,1,0:T(8,128)(2,1)}, u32[]{:S(2)}) copy-start(bf16[1,4096,256]{2,1,0:T(8,128)(2,1)} %param.16) | copy-start | bytes 6291460
  165.9 4.5 copy-start.13
  165.9 51.7 %all-to-all-start.6 = ((bf16[8,512,256]{2,1,0:T(8,128)(2,1)}), bf16[8,512,256]{2,1,0:T(8,128)(2,1)}, u32[]{:S(2)}, u32[]{:S(2)}) async-start(bf16[8,512,256]{2,1,0:T(8,128)(2,1)} %bitcast.90), calls=%async_computation.6 | async-start | bytes 4194304 | tf_op jit(solution)/shard_map/all_to_all | solution.py:49
  381.4 4.5 copy-start.11
  381.4 51.7 %all-to-all-start.1 = ((bf16[8,512,256]{2,1,0:T(8,128)(2,1)}), bf16[8,512,256]{2,1,0:T(8,128)(2,1)}, u32[]{:S(2)}, u32[]{:S(2)}) async-start(bf16[8,512,256]{2,1,0:T(8,128)(2,1)} %get-tuple-element.13), calls=%async_computation.1 | async-start | bytes 4194304 | tf_op jit(solution)/shard_map/all_to_all | solution.py:55
  433.1 5.3 copy-start.8
  433.1 187.1 %all-to-all-start.8 = ((bf16[8,128,4096]{2,1,0:T(8,128)(2,1)}), bf16[8,128,4096]{2,1,0:T(8,128)(2,1)}, u32[]{:S(2)}, u32[]{:S(2)}) async-start(bf16[8,128,4096]{2,1,0:T(8,128)(2,1)} %bitcast.84), calls=%async_computation.8 | async-start | bytes 16777216 | tf_op jit(solution)/shard_map/all_to_all | solution.py:86
  438.2 182.0 %all-gather.2.cloned.1.call-start = ((), (), s32[]{:S(2)}) async-start(), calls=%async_computation.10 | async-start | bytes 10485760 | tf_op jit(solution)/shard_map/all_gather | solution.py:97
  438.4 1.6 copy-start.7
  440.0 2.1 copy-start.2
  440.0 4.1 copy-start.6
  442.1 1.9 copy-start.4
  635.5 52.1 %all-to-all-start.9 = ((bf16[8,128,1024]{2,1,0:T(8,128)(2,1)}), bf16[8,128,1024]{2,1,0:T(8,128)(2,1)}, u32[]{:S(2)}, u32[]{:S(2)}) async-start(bf16[8,128,1024]{2,1,0:T(8,128)(2,1)} %bitcast.91), calls=%async_computation.9 | async-start | bytes 4194304 | tf_op jit(solution)/shard_map/all_to_all | solution.py:102
  639.8 2.8 copy-start.5
  642.0 2.4 copy-start.3
  644.3 43.2 %copy-start.12 = (f32[256,2]{0,1:T(2,128)S(1)}, f32[256,2]{0,1:T(2,128)}, u32[]{:S(2)}) copy-start(f32[256,2]{0,1:T(2,128)} %param.12) | copy-start | bytes 6148
  687.5 4.0 copy-start.1
Sparse Core Ops, SparseCore 0:
  450.3 60.5 all-gather.1
where the time goes:
time: 699 us; the launch traced here: 698 us
  blocking collectives  313 us (45%)
  waiting for transfers between devices  284 us (41%)
  matrix products  24.9 us (4%)
  local copies, waits for them, and re-layouts  22.1 us (3%)
  other arithmetic  21.1 us (3%)
  starting transfers between devices  18.6 us (3%)
  between operations  14.3 us (2%)
    all_to_all x1, waiting for transfers between devices, shards(): lax.all_to_all(outgoing.reshape(experts, capacity, width), 'expert', spli...  170 us
    all_to_all x1, blocking collectives, shards(): lax.all_to_all(to_pieces(expert_weights[0], experts), 'expert', split_axi...  55.9 us
    all_to_all x1, blocking collectives, shards(): lax.all_to_all(chosen[3], 'expert', split_axis=0, concat_axis=0, tiled=True)  51.9 us
    all_to_all x1, blocking collectives, shards(): lax.all_to_all(to_pieces(grads[0], experts), 'expert', split_axis=0, conc...  51.6 us
    all_to_all x1, blocking collectives, shards(): lax.all_to_all(chosen[2], 'expert', split_axis=0, concat_axis=0, tiled=True)  51.5 us
    all_to_all x1, blocking collectives, shards(): lax.all_to_all(to_pieces(first_moment[0], experts), 'expert', split_axis=...  51.2 us
    all_to_all x1, blocking collectives, shards(): lax.all_to_all(chosen[1], 'expert', split_axis=0, concat_axis=0, tiled=True)  51.2 us
    all_to_all x1, waiting for transfers between devices, shards(): lax.all_to_all(chosen[0], 'expert', split_axis=0, concat_axis=0, tiled=True)  39 us
  transfers between devices with their start and end apart: 5, of which 4 were waited for; matrix products, arithmetic and copies ran while one was open for 5% of the time, Pallas kernels for 0%

commit v1 on v0

v1 whole, which is shorter than its diff:
```python
import itertools

import jax
import jax.numpy as jnp
from jax import lax
from jax.sharding import PartitionSpec as P

beta_one = 0.9
beta_two = 0.999
learn_rate = 0.008
adam_eps = 1e-08

CORES = 2


def first_of(gradient, first):
    return beta_one * first.astype(jnp.float32) + (1.0 - beta_one) * gradient.astype(jnp.float32)


def second_of(gradient, second):
    grad_wide = gradient.astype(jnp.float32)
    return beta_two * second.astype(jnp.float32) + (1.0 - beta_two) * grad_wide * grad_wide


def updated_of(weight, gradient, first, second):
    return (
        weight.astype(jnp.float32)
        - learn_rate * first_of(gradient, first) / (jnp.sqrt(second_of(gradient, second)) + adam_eps)
    ).astype(jnp.bfloat16)


def grid_of(experts):
    columns = 1 << ((experts.bit_length() - 1) // 2)
    return experts // columns, columns


def swap(axis, mask, value):
    count = lax.axis_size(axis)
    return lax.ppermute(value, axis, [(i, i ^ mask) for i in range(count)])


def spread(axis, masks, blocks):
    return blocks + [swap(axis, mask, block) for mask in masks for block in blocks]


def pick(index, choices):
    out = choices[0]
    for at, choice in enumerate(choices[1:], 1):
        out = jnp.where(index == at, choice, out)
    return out


def gather_layers(block, layers, columns, z):
    ups, downs = [], []
    up = down = block
    for step in range(1, layers):
        up = lax.ppermute(
            up,
            "expert",
            [(k * columns + x, (k + 1) * columns + x) for k in range(step - 1, layers - 1) for x in range(columns)],
        )
        down = lax.ppermute(
            down,
            "expert",
            [((k + 1) * columns + x, k * columns + x) for k in range(layers - step) for x in range(columns)],
        )
        ups.append(up)
        downs.append(down)
    held = []
    for k in range(layers):
        near = sorted((o for o in range(layers) if o != k), key=lambda o: (abs(o - k), o))
        held.append([k] + near)
    slots = [block]
    for at in range(1, layers):
        groups = {}
        for k in range(layers):
            o = held[k][at]
            key = ("up", k - o) if o < k else ("down", o - k)
            groups.setdefault(key, []).append(k)
        parts = [(ups if key[0] == "up" else downs)[key[1] - 1] for key in groups]
        out = parts[0]
        for part, members in zip(parts[1:], list(groups.values())[1:]):
            here = jnp.zeros((), bool)
            for k in members:
                here = here | (z == k)
            out = jnp.where(here, part, out)
        slots.append(out)
    layer_in = [sum(jnp.where(z == k, held[k][at], 0) for k in range(layers)) for at in range(layers)]
    return slots, layer_in


def at_index(vector, index):
    index = jnp.asarray(index)
    places = jnp.arange(vector.shape[0], dtype=jnp.int32)
    return jnp.sum(jnp.where(index[..., None] == places, vector, 0), axis=-1)


def two_rounds(placement, hosting, layers):
    ids = jnp.arange(2 * layers, dtype=jnp.int32)
    beside = at_index(placement, hosting ^ 1)
    step = at_index(beside, ids ^ 1)
    lowest, reach = ids, ids
    for _ in range(layers - 1):
        reach = at_index(step, reach)
        lowest = jnp.minimum(lowest, reach)
    late = (lowest > at_index(lowest, ids ^ 1)).astype(jnp.int32)
    late_pairs = late.reshape(layers, 2)
    host_pairs = hosting.reshape(layers, 2)
    rounds = []
    for turn in (0, 1):
        column = jnp.where(late_pairs[:, 0] == turn, 0, 1)
        host = jnp.where(column == 0, host_pairs[:, 0], host_pairs[:, 1])
        rounds.append((column, host // 2, host % 2))
    return rounds


def migrate_by_rounds(moments, placement, hosting, layers, z, x):
    perms = list(itertools.permutations(range(layers)))
    table = jnp.array(perms, jnp.int32)

    def branch(perm):
        pairs = [(2 * k + c, 2 * perm[k] + c) for k in range(layers) for c in (0, 1) if perm[k] != k]
        if not pairs:
            return lambda block: block
        return lambda block: lax.ppermute(block, "expert", pairs)

    branches = [branch(perm) for perm in perms]
    rounds = two_rounds(placement, hosting, layers)
    numbers, stays = [], []
    for _, target, _ in rounds:
        match = jnp.all(table == target[None, :], axis=1)
        numbers.append(jnp.sum(jnp.where(match, jnp.arange(len(perms), dtype=jnp.int32), 0)))
        stays.append(at_index(target, z) == z)
    mine_first = at_index(rounds[0][0], z) == x
    arriving = jnp.sum(jnp.where(rounds[0][1] == z, rounds[0][2], 0))
    first_is_mine = arriving == x
    results = []
    for moment in moments:
        rows = moment.shape[0] // 2
        kept = lax.dynamic_slice_in_dim(moment, x * rows, rows, axis=0)
        given = lax.dynamic_slice_in_dim(moment, (1 - x) * rows, rows, axis=0)
        taken = swap("expert", 1, given)
        blocks = (jnp.where(mine_first, kept, taken), jnp.where(mine_first, taken, kept))
        landed = []
        for block, number, stay in zip(blocks, numbers, stays):
            landed.append(jnp.where(stay, block, lax.switch(number, branches, block)))
        own = jnp.where(first_is_mine, landed[0], landed[1])
        other = swap("expert", 1, jnp.where(first_is_mine, landed[1], landed[0]))
        top = jnp.where(x == 0, own, other)
        bottom = jnp.where(x == 0, other, own)
        results.append(jnp.concatenate([top, bottom], axis=0))
    return results


def migrate_by_pieces(moments, placement, experts):
    results = []
    for moment in moments:
        pieces = moment.reshape(experts, moment.shape[0] // experts, moment.shape[1])
        pieces = lax.all_to_all(pieces, "expert", split_axis=0, concat_axis=0, tiled=True)
        pieces = jnp.take(pieces, placement, axis=0)
        pieces = lax.all_to_all(pieces, "expert", split_axis=0, concat_axis=0, tiled=True)
        results.append(pieces.reshape(moment.shape))
    return results


def shards(
    tokens, routes, route_weights, placement, expert_weights, grads, first_moment, second_moment
):
    experts = lax.axis_size("expert")
    layers, columns = grid_of(experts)
    dp_count = lax.axis_size("dp")
    me = lax.axis_index("expert")
    z, x = me // columns, me % columns
    dp_index = lax.axis_index("dp")
    expert_ids = jnp.arange(experts, dtype=jnp.int32)
    tok_count = tokens.shape[0]
    shard = expert_weights.shape[2]

    updated = updated_of(expert_weights[0], grads[0], first_moment[0], second_moment[0])
    first_low = first_of(grads[0], first_moment[0]).astype(jnp.bfloat16)
    second_low = second_of(grads[0], second_moment[0]).astype(jnp.bfloat16)

    hosting = jnp.sum(
        jnp.where(placement[None, :] == expert_ids[:, None], expert_ids[None, :], 0), axis=1
    )

    slots, layer_in = gather_layers(updated, layers, columns, z)

    moments = (first_low, second_low)
    if columns == 2 and layers == 4:
        new_first, new_second = migrate_by_rounds(moments, placement, hosting, layers, z, x)
    else:
        new_first, new_second = migrate_by_pieces(moments, placement, experts)

    def held_block(owner):
        source = at_index(placement, owner)
        slot = sum(jnp.where(layer_in[at] == source // columns, at, 0) for at in range(layers))
        return pick(slot, slots)

    source_column = at_index(placement, me) % columns
    new_weights = held_block(me)
    for mask in range(1, columns):
        came = swap("expert", mask, held_block(me ^ mask))
        new_weights = jnp.where(source_column == (x ^ mask), came, new_weights)

    x_masks = list(range(1, columns))
    y_masks = [CORES * k for k in range(1, dp_count // CORES)]
    named = jnp.sum(
        jnp.where(routes[:, :, None] == expert_ids[None, None, :], route_weights[:, :, None], 0.0), axis=1
    )
    half = tok_count // 2
    upper = spread("expert", x_masks, [tokens[:half]])
    upper = spread("dp", y_masks, upper)
    lower = spread("dp", y_masks, [tokens[half:]])
    lower = spread("expert", x_masks, lower)
    y_count = dp_count // CORES
    lower = [lower[xs * y_count + ys] for ys in range(y_count) for xs in range(columns)]
    near = jnp.concatenate([part for pair in zip(upper, lower) for part in pair], axis=0)
    factors = jnp.concatenate(spread("dp", y_masks, spread("expert", x_masks, [named])), axis=0)

    partial = []
    for rows, scale in ((near, factors), (swap("dp", 1, near), swap("dp", 1, factors))):
        summed = 0.0
        for slot, layer in zip(slots, layer_in):
            act = jax.nn.silu(jnp.dot(rows, slot, preferred_element_type=jnp.float32)).astype(jnp.bfloat16)
            factor = jnp.sum(jnp.where(expert_ids[None, :] == layer * columns + x, scale, 0.0), axis=1)
            summed = summed + factor[:, None] * act.astype(jnp.float32)
        partial.append(summed)
    partial = jnp.concatenate(partial, axis=0)
    partial = partial.reshape(dp_count, columns, tok_count, shard)
    total = partial[:, 0]
    for mask in x_masks:
        total = total + swap("expert", mask, partial[:, mask].astype(jnp.bfloat16)).astype(jnp.float32)
    total = total.astype(jnp.bfloat16)
    pieces = [None] * dp_count
    for core in range(CORES):
        for ys in range(y_count):
            mask = ys * CORES + core
            piece = total[core * y_count + ys]
            pieces[mask] = piece if mask == 0 else swap("dp", mask, piece)
    bit = 1
    while bit < dp_count:
        turned = (dp_index & bit) != 0
        pieces = [jnp.where(turned, pieces[i ^ bit], pieces[i]) for i in range(dp_count)]
        bit *= 2
    mixed = jnp.concatenate(pieces, axis=1)
    return (new_weights[None], new_first[None], new_second[None], mixed)


def solution(mesh):
    return jax.shard_map(
        shards,
        mesh=mesh,
        in_specs=(
            P(("dp", "expert"), None),
            P(("dp", "expert"), None),
            P(("dp", "expert"), None),
            P(),
            P("expert", None, "dp"),
            P("expert", None, "dp"),
            P("expert", None, "dp"),
            P("expert", None, "dp"),
        ),
        out_specs=(
            P("expert", None, "dp"),
            P("expert", None, "dp"),
            P("expert", None, "dp"),
            P(("dp", "expert"), None),
        ),
        check_vma=False,
    )
```

time: 699 us -> 367 us (0.53)
  blocking collectives: 313 us -> 0 us
  waiting for transfers between devices: 284 us -> 226 us
  starting transfers between devices: 18.6 us -> 49.3 us
  other arithmetic: 21.1 us -> 33.3 us
  matrix products: 24.9 us -> 33.3 us
    all_to_all x6 -> x0, blocking collectives: 313 us -> none  [the longest x1 55.9 us: shards(): lax.all_to_all(to_pieces(expert_weights[0], experts), 'expert', split_axi...]
    all_to_all x4 -> x0, waiting for transfers between devices: 284 us -> none  [the longest x1 170 us: shards(): lax.all_to_all(outgoing.reshape(experts, capacity, width), 'expert', spli...]
    ppermute x0 -> x30, waiting for transfers between devices: none -> 226 us  [the longest x20 132 us: swap(): return lax.ppermute(value, axis, [(i, i ^ mask) for i in range(count)])]
    ppermute x0 -> x30, starting transfers between devices: none -> 49.3 us  [the longest x20 22.8 us: swap(): return lax.ppermute(value, axis, [(i, i ^ mask) for i in range(count)])]
    all_to_all x4 -> x0, starting transfers between devices: 18.4 us -> none  [the longest x1 5.07 us: shards(): lax.all_to_all(outgoing.reshape(experts, capacity, width), 'expert', spli...]
    gather x4 -> x0, local copies, waits for them, and re-layouts: 14.4 us -> none  [shards(): chosen = tuple((jnp.take(member, placement, axis=0) for member in spread))]
    select_n x2 -> x8, other arithmetic: 5.58 us -> 16.4 us  [the longest x2 6.97 us: migrate_by_rounds(): other = swap('expert', 1, jnp.where(first_is_mine, landed[1], landed[0]))]
    dot_general x3 -> x8, matrix products: 24.9 us -> 33.3 us  [shards(): jnp.dot(rows, slot, preferred_element_type=jnp.float32)]
  transfers between devices with their start and end apart: 5 -> 30, of which waited for: 4 -> 16; matrix products, arithmetic and copies ran while one was open for 5% -> 22% of each run, Pallas kernels for 0% -> 0%
where the time goes in v1:
time: 367 us; the launch traced here: 369 us
  waiting for transfers between devices  226 us (62%)
  starting transfers between devices  49.3 us (13%)
  other arithmetic  33.3 us (9%)
  matrix products  33.3 us (9%)
  local copies, waits for them, and re-layouts  16.3 us (4%)
  between operations  9.83 us (3%)
    ppermute x20, waiting for transfers between devices, swap(): return lax.ppermute(value, axis, [(i, i ^ mask) for i in range(count)])  132 us
    ppermute x4, waiting for transfers between devices, branch(): return lambda block: lax.ppermute(block, 'expert', pairs)  91.4 us
    dot_general x8, matrix products, shards(): jnp.dot(rows, slot, preferred_element_type=jnp.float32)  33.3 us
    ppermute x20, starting transfers between devices, swap(): return lax.ppermute(value, axis, [(i, i ^ mask) for i in range(count)])  22.8 us
    ppermute x4, starting transfers between devices, branch(): return lambda block: lax.ppermute(block, 'expert', pairs)  13.6 us
    unnamed x34, local copies, waits for them, and re-layouts  10.7 us
    ppermute x3, starting transfers between devices, gather_layers(): lax.ppermute(up, 'expert', [(k * columns + x, (k + 1) * columns + x) for...  9.08 us
  transfers between devices with their start and end apart: 30, of which 16 were waited for; matrix products, arithmetic and copies ran while one was open for 22% of the time, Pallas kernels for 0%

profile of v1, /device:TPU:0, one launch (start us, length us, event | category | flops | bytes accessed | tf_op | source)
XLA Modules:
  0.0 368.5 jit_solution(16208677555466798816)
XLA Ops:
  1.3 3.0 collective-permute-start.103
  5.8 6.8 %fusion.4 = (bf16[4096,256]{1,0:T(8,128)(2,1)}, bf16[4096,256]{1,0:T(8,128)(2,1)S(1)}, bf16[4096,256]{1,0:T(8,128)(2,1)}) fusion(bf16[1,4096,256]{2,1,0:T(8,128)(2,1)} %param.112, bf16[1,4096,256]{2,1,0:T(8,128)(2,1)} %param.110, bf16[1,4096,256]{2,1,0:T(8,128)(2,1)} %param.111, bf16[1,4096,256]{2,1,0:T(8,128)(2,1)} %param.109), kind=kLoop, calls=%fused_computation.8 | loop fusion | flops 18874368 | bytes 14680064 | tf_op jit(solution)/shard_map/convert_element_type | solution.py:181
  12.7 5.0 %collective-permute-start.92 = (bf16[4096,256]{1,0:T(8,128)(2,1)S(1)}, bf16[4096,256]{1,0:T(8,128)(2,1)}, u32[]{:S(2)}, u32[]{:S(2)}) collective-permute-start(bf16[4096,256]{1,0:T(8,128)(2,1)S(1)} %get-tuple-element.233), channel_id=1, source_target_pairs={{0,2},{1,3},{2,4},{3,5},{4,6},{5,7},{8,10},{9,11},{10,12},{11,13},... | collective-permute-start | bytes 6291464 | tf_op jit(solution)/shard_map/ppermute | solution.py:57
  23.0 2.4 constant_dynamic-slice_fusion
  35.9 9.6 %collective-permute-done.106 = bf16[128,4096]{1,0:T(8,128)(2,1)} collective-permute-done((bf16[128,4096]{1,0:T(8,128)(2,1)}, bf16[128,4096]{1,0:T(8,128)(2,1)}, u32[]{:S(2)}, u32[]{:S(2)}) %collective-permute-start.106) | collective-permute-done | bytes 1048608 | tf_op jit(solution)/shard_map/ppermute | solution.py:39
  46.0 2.4 constant_dynamic-update-slice_fusion.5
  48.4 17.5 %collective-permute-done.107 = bf16[128,4096]{1,0:T(8,128)(2,1)} collective-permute-done((bf16[128,4096]{1,0:T(8,128)(2,1)}, bf16[128,4096]{1,0:T(8,128)(2,1)}, u32[]{:S(2)}, u32[]{:S(2)}) %collective-permute-start.107) | collective-permute-done | bytes 1048608 | tf_op jit(solution)/shard_map/ppermute | solution.py:39
  67.3 2.4 constant_dynamic-update-slice_fusion.4
  69.7 1.9 collective-permute-start.101
  71.6 11.6 %collective-permute-done.109 = bf16[128,4096]{1,0:T(8,128)(2,1)S(1)} collective-permute-done((bf16[128,4096]{1,0:T(8,128)(2,1)}, bf16[128,4096]{1,0:T(8,128)(2,1)S(1)}, u32[]{:S(2)}, u32[]{:S(2)}) %collective-permute-start.109) | collective-permute-done | bytes 1048608 | tf_op jit(solution)/shard_map/ppermute | solution.py:39
  87.3 2.1 collective-permute-start.93
  89.5 13.3 %collective-permute-done.110 = bf16[128,4096]{1,0:T(8,128)(2,1)S(1)} collective-permute-done((bf16[128,4096]{1,0:T(8,128)(2,1)}, bf16[128,4096]{1,0:T(8,128)(2,1)S(1)}, u32[]{:S(2)}, u32[]{:S(2)}) %collective-permute-start.110) | collective-permute-done | bytes 1048608 | tf_op jit(solution)/shard_map/ppermute | solution.py:39
  105.1 13.0 %collective-permute-done.111 = bf16[128,4096]{1,0:T(8,128)(2,1)S(1)} collective-permute-done((bf16[128,4096]{1,0:T(8,128)(2,1)S(1)}, bf16[128,4096]{1,0:T(8,128)(2,1)S(1)}, u32[]{:S(2)}, u32[]{:S(2)}) %collective-permute-start.111) | collective-permute-done | bytes 1048608 | tf_op jit(solution)/shard_map/ppermute | solution.py:39
  119.7 20.4 %collective-permute-done.99 = bf16[2048,256]{1,0:T(8,128)(2,1)S(1)} collective-permute-done((bf16[2048,256]{1,0:T(8,128)(2,1)S(1)}, bf16[2048,256]{1,0:T(8,128)(2,1)S(1)}, u32[]{:S(2)}, u32[]{:S(2)}) %collective-permute-start.99) | collective-permute-done | bytes 1048608 | tf_op jit(solution)/shard_map/ppermute | solution.py:39
  140.1 2.0 broadcast_select_fusion.3
  143.0 29.5 %conditional.4 = (bf16[2048,256]{1,0:T(8,128)(2,1)}) conditional(s32[]{:T(128)} %clamp.8, bf16[2048,256]{1,0:T(8,128)(2,1)S(1)} %get-tuple-element.257, bf16[2048,256]{1,0:T(8,128)(2,1)S(1)} %get-tuple-element.257, bf16[2048,256]{1,0:T(8,128)(2,1)S(1)} %get-tuple-element.257, ...), branch_computations={%region_14.15_spmd, %region_15.16_spmd, %region_16.17_spmd, %regio... | conditional | bytes 4194352 | solution.py:146
  143.0 5.4 %collective-permute-start.18 = (bf16[2048,256]{1,0:T(8,128)(2,1)S(1)}, bf16[2048,256]{1,0:T(8,128)(2,1)}, u32[]{:S(2)}, u32[]{:S(2)}) collective-permute-start(bf16[2048,256]{1,0:T(8,128)(2,1)S(1)} %param.19), channel_id=1, source_target_pairs={{0,6},{1,7},{2,0},{3,1},{6,2},{7,3},{8,14},{9,15},{10,8},{11,9},{1... | collective-permute-start | bytes 3145736 | tf_op jit(solution)/shard_map/cond/branch_19_fun/ppermute | solution.py:125
  148.5 24.1 %collective-permute-done.18 = bf16[2048,256]{1,0:T(8,128)(2,1)} collective-permute-done((bf16[2048,256]{1,0:T(8,128)(2,1)S(1)}, bf16[2048,256]{1,0:T(8,128)(2,1)}, u32[]{:S(2)}, u32[]{:S(2)}) %collective-permute-start.18) | collective-permute-done | bytes 1048608 | tf_op jit(solution)/shard_map/cond/branch_19_fun/ppermute | solution.py:125
  172.5 25.4 %conditional.6 = (bf16[2048,256]{1,0:T(8,128)(2,1)}) conditional(s32[]{:T(128)} %clamp.8, bf16[2048,256]{1,0:T(8,128)(2,1)} %get-tuple-element.238, bf16[2048,256]{1,0:T(8,128)(2,1)} %get-tuple-element.238, bf16[2048,256]{1,0:T(8,128)(2,1)} %get-tuple-element.238, bf16[2048,256]{1,0:T(8,128)(2,1)} %get-tuple-element.238, ...), branch_computations={%region_65.66_spmd, %region_66.67_spmd, %region_67.68_spmd, %regio... | conditional | bytes 4194352 | solution.py:146
  172.5 4.1 %collective-permute-start.64 = (bf16[2048,256]{1,0:T(8,128)(2,1)}, bf16[2048,256]{1,0:T(8,128)(2,1)}, u32[]{:S(2)}, u32[]{:S(2)}) collective-permute-start(bf16[2048,256]{1,0:T(8,128)(2,1)} %param.67), channel_id=1, source_target_pairs={{0,6},{1,7},{2,0},{3,1},{6,2},{7,3},{8,14},{9,15},{10,8},{11,9},{1... | collective-permute-start | bytes 3145736 | tf_op jit(solution)/shard_map/cond/branch_19_fun/ppermute | solution.py:125
  176.6 21.3 %collective-permute-done.64 = bf16[2048,256]{1,0:T(8,128)(2,1)} collective-permute-done((bf16[2048,256]{1,0:T(8,128)(2,1)}, bf16[2048,256]{1,0:T(8,128)(2,1)}, u32[]{:S(2)}, u32[]{:S(2)}) %collective-permute-start.64) | collective-permute-done | bytes 1048608 | tf_op jit(solution)/shard_map/cond/branch_19_fun/ppermute | solution.py:125
  197.9 25.6 %conditional.5 = (bf16[2048,256]{1,0:T(8,128)(2,1)}) conditional(s32[]{:T(128)} %clamp.9, bf16[2048,256]{1,0:T(8,128)(2,1)} %get-tuple-element.258, bf16[2048,256]{1,0:T(8,128)(2,1)} %get-tuple-element.258, bf16[2048,256]{1,0:T(8,128)(2,1)} %get-tuple-element.258, bf16[2048,256]{1,0:T(8,128)(2,1)} %get-tuple-element.258, ...), branch_computations={%region_41.42_spmd, %region_42.43_spmd, %region_43.44_spmd, %regio... | conditional | bytes 4194352 | solution.py:146
  197.9 1.9 collective-permute-start.36
  199.8 23.7 %collective-permute-done.36 = bf16[2048,256]{1,0:T(8,128)(2,1)} collective-permute-done((bf16[2048,256]{1,0:T(8,128)(2,1)}, bf16[2048,256]{1,0:T(8,128)(2,1)}, u32[]{:S(2)}, u32[]{:S(2)}) %collective-permute-start.36) | collective-permute-done | bytes 1048608 | tf_op jit(solution)/shard_map/cond/branch_14_fun/ppermute | solution.py:125
  223.5 24.5 %conditional.7 = (bf16[2048,256]{1,0:T(8,128)(2,1)}) conditional(s32[]{:T(128)} %clamp.9, bf16[2048,256]{1,0:T(8,128)(2,1)S(1)} %get-tuple-element.237, bf16[2048,256]{1,0:T(8,128)(2,1)S(1)} %get-tuple-element.237, bf16[2048,256]{1,0:T(8,128)(2,1)S(1)} %get-tuple-element.237, ...), branch_computations={%region_89.90_spmd, %region_90.91_spmd, %region_91.92_spmd, %regio... | conditional | bytes 4194352 | solution.py:146
  223.5 2.2 collective-permute-start.82
  225.7 22.3 %collective-permute-done.82 = bf16[2048,256]{1,0:T(8,128)(2,1)} collective-permute-done((bf16[2048,256]{1,0:T(8,128)(2,1)S(1)}, bf16[2048,256]{1,0:T(8,128)(2,1)}, u32[]{:S(2)}, u32[]{:S(2)}) %collective-permute-start.82) | collective-permute-done | bytes 1048608 | tf_op jit(solution)/shard_map/cond/branch_14_fun/ppermute | solution.py:125
  248.1 3.5 broadcast_select_fusion.11
  253.1 2.0 collective-permute-start.94
  256.3 3.4 broadcast_select_fusion.9
  266.5 11.5 %collective-permute-done.100 = bf16[2048,256]{1,0:T(8,128)(2,1)} collective-permute-done((bf16[2048,256]{1,0:T(8,128)(2,1)}, bf16[2048,256]{1,0:T(8,128)(2,1)}, u32[]{:S(2)}, u32[]{:S(2)}) %collective-permute-start.100) | collective-permute-done | bytes 1048608 | tf_op jit(solution)/shard_map/ppermute | solution.py:39
  278.0 1.9 broadcast_select_fusion.16
  279.9 15.2 %collective-permute-done.102 = bf16[2048,256]{1,0:T(8,128)(2,1)} collective-permute-done((bf16[2048,256]{1,0:T(8,128)(2,1)}, bf16[2048,256]{1,0:T(8,128)(2,1)}, u32[]{:S(2)}, u32[]{:S(2)}) %collective-permute-start.102) | collective-permute-done | bytes 1048608 | tf_op jit(solution)/shard_map/ppermute | solution.py:39
  296.7 3.5 collective-permute-done.97
  300.1 3.8 %select_select_fusion = (bf16[4096,256]{1,0:T(8,128)(2,1)S(1)}, bf16[4096,256]{1,0:T(8,128)(2,1)S(1)}, bf16[4096,256]{1,0:T(8,128)(2,1)S(1)}, bf16[4096,256]{1,0:T(8,128)(2,1)S(1)}) fusion(bf16[4096,256]{1,0:T(8,128)(2,1)S(1)} %get-tuple-element.233, pred[]{:T(512)S(6)} %eq.358, pred[]{:T(512)S(6)} %eq.357, pred[]{:T(512)S(6)} %eq.356, ...), kind=kLoop, calls=%fused_computation.13 | loop fusion | flops 9437184 | bytes 23068680 | tf_op jit(solution)/shard_map/jit(_where)/select_n | solution.py:49
  304.6 2.3 fusion.13
  306.9 2.3 fusion.14
  309.3 2.3 fusion.15
  311.6 3.6 multiply_add_fusion.1
  315.2 5.7 %fusion.16 = f32[1024,256]{1,0:T(8,128)S(1)} fusion(bf16[1024,4096]{1,0:T(8,128)(2,1)} %collective-permute-done.113, bf16[4096,256]{1,0:T(8,128)(2,1)S(1)} %get-tuple-element.229), kind=kOutput, calls=%fused_computation.137 | convolution fusion | flops 2147483648 | bytes 11534336 | tf_op jit(solution)/shard_map/dot_general | solution.py:225
  320.9 5.7 %fusion.17 = f32[1024,256]{1,0:T(8,128)S(1)} fusion(bf16[1024,4096]{1,0:T(8,128)(2,1)} %collective-permute-done.113, bf16[4096,256]{1,0:T(8,128)(2,1)S(1)} %get-tuple-element.230), kind=kOutput, calls=%fused_computation.138 | convolution fusion | flops 2147483648 | bytes 11534336 | tf_op jit(solution)/shard_map/dot_general | solution.py:225
  326.7 5.7 %fusion.18 = f32[1024,256]{1,0:T(8,128)S(1)} fusion(bf16[1024,4096]{1,0:T(8,128)(2,1)} %collective-permute-done.113, bf16[4096,256]{1,0:T(8,128)(2,1)S(1)} %get-tuple-element.231), kind=kOutput, calls=%fused_computation.139 | convolution fusion | flops 2147483648 | bytes 11534336 | tf_op jit(solution)/shard_map/dot_general | solution.py:225
  332.4 5.6 %multiply_add_fusion = f32[1024,256]{1,0:T(8,128)S(1)} fusion(f32[1024,256]{1,0:T(8,128)S(1)} %fusion.16, f32[1024,256]{1,0:T(8,128)S(1)} %fusion.17, f32[1024,256]{1,0:T(8,128)S(1)} %fusion.18, f32[1024]{0:T(1024)S(1)} %get-tuple-element.204, f32[1024]{0:T(1024)S(1)} %get-tuple-element.205, f32[1024]{0:T(1024)S(1)} %get-tuple-element.206, ...), kind=kOutput, calls=%fused_computation.21 | convolution fusion | flops 2155610112 | bytes 14696448 | tf_op jit(solution)/shard_map/dot_general | solution.py:225
  342.6 14.6 %collective-permute-done.114 = bf16[4,256,256]{2,1,0:T(8,128)(2,1)S(1)} collective-permute-done((bf16[4,256,256]{2,1,0:T(8,128)(2,1)S(1)}, bf16[4,256,256]{2,1,0:T(8,128)(2,1)S(1)}, u32[]{:S(2)}, u32[]{:S(2)}) %collective-permute-start.114) | collective-permute-done | bytes 524320 | tf_op jit(solution)/shard_map/ppermute | solution.py:39
  357.4 1.7 collective-permute-start.115
  359.1 1.9 collective-permute-start.116
  361.0 1.8 select_bitcast_fusion
  364.3 3.3 collective-permute-done.116
  (107 shorter events, 39.0 us)
Async XLA Ops:
  1.3 16.3 %copy-start.5 = (bf16[256,4096]{1,0:T(8,128)(2,1)S(1)}, bf16[256,4096]{1,0:T(8,128)(2,1)}, u32[]{:S(2)}) copy-start(bf16[256,4096]{1,0:T(8,128)(2,1)} %param.105) | copy-start | bytes 6291460
  1.3 26.9 %collective-permute-start.103 = (f32[256,8]{0,1:T(8,128)S(1)}, f32[256,8]{0,1:T(8,128)S(1)}, u32[]{:S(2)}, u32[]{:S(2)}) collective-permute-start(f32[256,8]{0,1:T(8,128)S(1)} %select_reduce_fusion.8), channel_id=1, source_target_pairs={{0,1},{1,0},{2,3},{3,2},{4,5},{5,4},{6,7},{7,6},{8,9},{9,8},{10,11... | collective-permute-start | bytes 24584 | tf_op jit(solution)/shard_map/ppermute | solution.py:39
  4.3 25.2 %collective-permute-start.104 = (f32[256,8]{0,1:T(8,128)S(1)}, f32[256,8]{0,1:T(8,128)S(1)}, u32[]{:S(2)}, u32[]{:S(2)}) collective-permute-start(f32[256,8]{0,1:T(8,128)S(1)} %select_reduce_fusion.8), channel_id=1, source_target_pairs={{0,16},{8,24},{16,0},{24,8},{1,17},{9,25},{17,1},{25,9},{2,18},{10... | collective-permute-start | bytes 24584 | tf_op jit(solution)/shard_map/ppermute | solution.py:39
  12.7 8.4 %copy-start.11 = (s32[8]{0:T(128)S(1)}, s32[8]{0:T(128)}, u32[]{:S(2)}) copy-start(s32[8]{0:T(128)} %param.108) | copy-start | bytes 100
  12.7 72.1 %collective-permute-start.92 = (bf16[4096,256]{1,0:T(8,128)(2,1)S(1)}, bf16[4096,256]{1,0:T(8,128)(2,1)}, u32[]{:S(2)}, u32[]{:S(2)}) collective-permute-start(bf16[4096,256]{1,0:T(8,128)(2,1)S(1)} %get-tuple-element.233), channel_id=1, source_target_pairs={{0,2},{1,3},{2,4},{3,5},{4,6},{5,7},{8,10},{9,11},{10,12},{11,13},... | collective-permute-start | bytes 6291464 | tf_op jit(solution)/shard_map/ppermute | solution.py:57
  19.1 26.4 %collective-permute-start.106 = (bf16[128,4096]{1,0:T(8,128)(2,1)}, bf16[128,4096]{1,0:T(8,128)(2,1)}, u32[]{:S(2)}, u32[]{:S(2)}) collective-permute-start(bf16[128,4096]{1,0:T(8,128)(2,1)} %get-tuple-element.244), channel_id=1, source_target_pairs={{0,1},{1,0},{2,3},{3,2},{4,5},{5,4},{6,7},{7,6},{8,9},{9,8},{10,11... | collective-permute-start | bytes 3145736 | tf_op jit(solution)/shard_map/ppermute | solution.py:39
  19.6 46.3 %collective-permute-start.107 = (bf16[128,4096]{1,0:T(8,128)(2,1)}, bf16[128,4096]{1,0:T(8,128)(2,1)}, u32[]{:S(2)}, u32[]{:S(2)}) collective-permute-start(bf16[128,4096]{1,0:T(8,128)(2,1)} %get-tuple-element.243), channel_id=1, source_target_pairs={{0,1},{1,0},{2,3},{3,2},{4,5},{5,4},{6,7},{7,6},{8,9},{9,8},{10,11... | collective-permute-start | bytes 3145736 | tf_op jit(solution)/shard_map/ppermute | solution.py:39
  23.0 2.4 copy-start.3
  23.0 2.8 copy-start.6
  25.7 2.4 copy-start.10
  28.2 59.1 %collective-permute-start.95 = (bf16[4096,256]{1,0:T(8,128)(2,1)S(1)}, bf16[4096,256]{1,0:T(8,128)(2,1)}, u32[]{:S(2)}, u32[]{:S(2)}) collective-permute-start(bf16[4096,256]{1,0:T(8,128)(2,1)S(1)} %get-tuple-element.233), channel_id=1, source_target_pairs={{2,0},{3,1},{4,2},{5,3},{6,4},{7,5},{10,8},{11,9},{12,10},{13,11},... | collective-permute-start | bytes 6291464 | tf_op jit(solution)/shard_map/ppermute | solution.py:62
  29.5 4.8 %collective-permute-start.105 = (f32[256,8]{0,1:T(8,128)S(1)}, f32[256,8]{0,1:T(8,128)S(1)}, u32[]{:S(2)}, u32[]{:S(2)}) collective-permute-start(f32[256,8]{0,1:T(8,128)S(1)} %collective-permute-done.103), channel_id=1, source_target_pairs={{0,16},{8,24},{16,0},{24,8},{1,17},{9,25},{17,1},{25,9},{2,18},{10... | collective-permute-start | bytes 24584 | tf_op jit(solution)/shard_map/ppermute | solution.py:39
  34.3 35.3 %collective-permute-start.108 = (bf16[128,4096]{1,0:T(8,128)(2,1)}, bf16[128,4096]{1,0:T(8,128)(2,1)S(1)}, u32[]{:S(2)}, u32[]{:S(2)}) collective-permute-start(bf16[128,4096]{1,0:T(8,128)(2,1)} %get-tuple-element.244), channel_id=1, source_target_pairs={{0,16},{8,24},{16,0},{24,8},{1,17},{9,25},{17,1},{25,9},{2,18},{10... | collective-permute-start | bytes 3145736 | tf_op jit(solution)/shard_map/ppermute | solution.py:39
  45.5 37.7 %collective-permute-start.109 = (bf16[128,4096]{1,0:T(8,128)(2,1)}, bf16[128,4096]{1,0:T(8,128)(2,1)S(1)}, u32[]{:S(2)}, u32[]{:S(2)}) collective-permute-start(bf16[128,4096]{1,0:T(8,128)(2,1)} %get-tuple-element.243), channel_id=1, source_target_pairs={{0,16},{8,24},{16,0},{24,8},{1,17},{9,25},{17,1},{25,9},{2,18},{10... | collective-permute-start | bytes 3145736 | tf_op jit(solution)/shard_map/ppermute | solution.py:39
  46.0 23.7 %copy-start.9 = (bf16[2048,256]{1,0:T(8,128)(2,1)S(1)}, bf16[2048,256]{1,0:T(8,128)(2,1)}, u32[]{:S(2)}) copy-start(bf16[2048,256]{1,0:T(8,128)(2,1)} %constant_dynamic-slice_fusion) | copy-start | bytes 3145732
  65.9 36.8 %collective-permute-start.110 = (bf16[128,4096]{1,0:T(8,128)(2,1)}, bf16[128,4096]{1,0:T(8,128)(2,1)S(1)}, u32[]{:S(2)}, u32[]{:S(2)}) collective-permute-start(bf16[128,4096]{1,0:T(8,128)(2,1)} %collective-permute-done.106), channel_id=1, source_target_pairs={{0,16},{8,24},{16,0},{24,8},{1,17},{9,25},{17,1},{25,9},{2,18},{10... | collective-permute-start | bytes 3145736 | tf_op jit(solution)/shard_map/ppermute | solution.py:39
  69.7 49.5 %collective-permute-start.101 = (bf16[2048,256]{1,0:T(8,128)(2,1)S(1)}, bf16[2048,256]{1,0:T(8,128)(2,1)S(1)}, u32[]{:S(2)}, u32[]{:S(2)}) collective-permute-start(bf16[2048,256]{1,0:T(8,128)(2,1)S(1)} %copy-done.9), channel_id=1, source_target_pairs={{0,1},{1,0},{2,3},{3,2},{4,5},{5,4},{6,7},{7,6},{8,9},{9,8},{10,11... | collective-permute-start | bytes 3145736 | tf_op jit(solution)/shard_map/ppermute | solution.py:39
  83.2 35.0 %collective-permute-start.111 = (bf16[128,4096]{1,0:T(8,128)(2,1)S(1)}, bf16[128,4096]{1,0:T(8,128)(2,1)S(1)}, u32[]{:S(2)}, u32[]{:S(2)}) collective-permute-start(bf16[128,4096]{1,0:T(8,128)(2,1)S(1)} %collective-permute-done.109), channel_id=1, source_target_pairs={{0,1},{1,0},{2,3},{3,2},{4,5},{5,4},{6,7},{7,6},{8,9},{9,8},{10,11... | collective-permute-start | bytes 3145736 | tf_op jit(solution)/shard_map/ppermute | solution.py:39
  84.8 55.3 %collective-permute-start.99 = (bf16[2048,256]{1,0:T(8,128)(2,1)S(1)}, bf16[2048,256]{1,0:T(8,128)(2,1)S(1)}, u32[]{:S(2)}, u32[]{:S(2)}) collective-permute-start(bf16[2048,256]{1,0:T(8,128)(2,1)S(1)} %constant_dynamic-slice_fusion.1), channel_id=1, source_target_pairs={{0,1},{1,0},{2,3},{3,2},{4,5},{5,4},{6,7},{7,6},{8,9},{9,8},{10,11... | collective-permute-start | bytes 3145736 | tf_op jit(solution)/shard_map/ppermute | solution.py:39
  87.3 52.7 %copy-start.2 = (bf16[4096,256]{1,0:T(8,128)(2,1)S(1)}, bf16[4096,256]{1,0:T(8,128)(2,1)}, u32[]{:S(2)}) copy-start(bf16[4096,256]{1,0:T(8,128)(2,1)} %get-tuple-element.232) | copy-start | bytes 6291460
  87.3 52.7 %copy-start.4 = (bf16[4096,256]{1,0:T(8,128)(2,1)S(1)}, bf16[4096,256]{1,0:T(8,128)(2,1)}, u32[]{:S(2)}) copy-start(bf16[4096,256]{1,0:T(8,128)(2,1)} %get-tuple-element.234) | copy-start | bytes 6291460
  87.3 165.7 %collective-permute-start.93 = (bf16[4096,256]{1,0:T(8,128)(2,1)}, bf16[4096,256]{1,0:T(8,128)(2,1)}, u32[]{:S(2)}, u32[]{:S(2)}) collective-permute-start(bf16[4096,256]{1,0:T(8,128)(2,1)} %collective-permute-done.92), channel_id=1, source_target_pairs={{2,4},{3,5},{4,6},{5,7},{10,12},{11,13},{12,14},{13,15},{18,20},{1... | collective-permute-start | bytes 6291464 | tf_op jit(solution)/shard_map/ppermute | solution.py:57
  102.8 152.3 %collective-permute-start.96 = (bf16[4096,256]{1,0:T(8,128)(2,1)}, bf16[4096,256]{1,0:T(8,128)(2,1)}, u32[]{:S(2)}, u32[]{:S(2)}) collective-permute-start(bf16[4096,256]{1,0:T(8,128)(2,1)} %collective-permute-done.95), channel_id=1, source_target_pairs={{2,0},{3,1},{4,2},{5,3},{10,8},{11,9},{12,10},{13,11},{18,16},{19,... | collective-permute-start | bytes 6291464 | tf_op jit(solution)/shard_map/ppermute | solution.py:62
  118.1 141.7 %collective-permute-start.112 = (f32[1024,8]{0,1:T(8,128)S(1)}, f32[1024,8]{0,1:T(8,128)S(1)}, u32[]{:S(2)}, u32[]{:S(2)}) collective-permute-start(f32[1024,8]{0,1:T(8,128)S(1)} %pad_maximum_fusion.2), channel_id=1, source_target_pairs={{0,8},{8,0},{16,24},{24,16},{1,9},{9,1},{17,25},{25,17},{2,10},{10... | collective-permute-start | bytes 98312 | tf_op jit(solution)/shard_map/ppermute | solution.py:39
  119.2 196.0 %collective-permute-start.113 = (bf16[1024,4096]{1,0:T(8,128)(2,1)}, bf16[1024,4096]{1,0:T(8,128)(2,1)}, u32[]{:S(2)}, u32[]{:S(2)}) collective-permute-start(bf16[1024,4096]{1,0:T(8,128)(2,1)} %constant_dynamic-update-slice_fusion), channel_id=1, source_target_pairs={{0,8},{8,0},{16,24},{24,16},{1,9},{9,1},{17,25},{25,17},{2,10},{10... | collective-permute-start | bytes 25165832 | tf_op jit(solution)/shard_map/ppermute | solution.py:39
  142.1 1.0 copy-start.1
  143.0 29.5 %collective-permute-start.18 = (bf16[2048,256]{1,0:T(8,128)(2,1)S(1)}, bf16[2048,256]{1,0:T(8,128)(2,1)}, u32[]{:S(2)}, u32[]{:S(2)}) collective-permute-start(bf16[2048,256]{1,0:T(8,128)(2,1)S(1)} %param.19), channel_id=1, source_target_pairs={{0,6},{1,7},{2,0},{3,1},{6,2},{7,3},{8,14},{9,15},{10,8},{11,9},{1... | collective-permute-start | bytes 3145736 | tf_op jit(solution)/shard_map/cond/branch_19_fun/ppermute | solution.py:125
  172.5 25.4 %collective-permute-start.64 = (bf16[2048,256]{1,0:T(8,128)(2,1)}, bf16[2048,256]{1,0:T(8,128)(2,1)}, u32[]{:S(2)}, u32[]{:S(2)}) collective-permute-start(bf16[2048,256]{1,0:T(8,128)(2,1)} %param.67), channel_id=1, source_target_pairs={{0,6},{1,7},{2,0},{3,1},{6,2},{7,3},{8,14},{9,15},{10,8},{11,9},{1... | collective-permute-start | bytes 3145736 | tf_op jit(solution)/shard_map/cond/branch_19_fun/ppermute | solution.py:125
  197.9 25.6 %collective-permute-start.36 = (bf16[2048,256]{1,0:T(8,128)(2,1)}, bf16[2048,256]{1,0:T(8,128)(2,1)}, u32[]{:S(2)}, u32[]{:S(2)}) collective-permute-start(bf16[2048,256]{1,0:T(8,128)(2,1)} %param.38), channel_id=1, source_target_pairs={{0,4},{1,5},{4,0},{5,1},{8,12},{9,13},{12,8},{13,9},{16,20},{17,21... | collective-permute-start | bytes 3145736 | tf_op jit(solution)/shard_map/cond/branch_14_fun/ppermute | solution.py:125
  223.5 24.5 %collective-permute-start.82 = (bf16[2048,256]{1,0:T(8,128)(2,1)S(1)}, bf16[2048,256]{1,0:T(8,128)(2,1)}, u32[]{:S(2)}, u32[]{:S(2)}) collective-permute-start(bf16[2048,256]{1,0:T(8,128)(2,1)S(1)} %param.86), channel_id=1, source_target_pairs={{0,4},{1,5},{4,0},{5,1},{8,12},{9,13},{12,8},{13,9},{16,20},{17,21... | collective-permute-start | bytes 3145736 | tf_op jit(solution)/shard_map/cond/branch_14_fun/ppermute | solution.py:125
  248.1 8.3 %copy-start = (bf16[2048,256]{1,0:T(8,128)(2,1)S(1)}, bf16[2048,256]{1,0:T(8,128)(2,1)}, u32[]{:S(2)}) copy-start(bf16[2048,256]{1,0:T(8,128)(2,1)} %get-tuple-element.238) | copy-start | bytes 3145732
  251.6 26.4 %collective-permute-start.100 = (bf16[2048,256]{1,0:T(8,128)(2,1)}, bf16[2048,256]{1,0:T(8,128)(2,1)}, u32[]{:S(2)}, u32[]{:S(2)}) collective-permute-start(bf16[2048,256]{1,0:T(8,128)(2,1)} %get-tuple-element.222), channel_id=1, source_target_pairs={{0,1},{1,0},{2,3},{3,2},{4,5},{5,4},{6,7},{7,6},{8,9},{9,8},{10,11... | collective-permute-start | bytes 3145736 | tf_op jit(solution)/shard_map/ppermute | solution.py:39
  253.1 43.6 %collective-permute-start.94 = (bf16[4096,256]{1,0:T(8,128)(2,1)}, bf16[4096,256]{1,0:T(8,128)(2,1)}, u32[]{:S(2)}, u32[]{:S(2)}) collective-permute-start(bf16[4096,256]{1,0:T(8,128)(2,1)} %collective-permute-done.93), channel_id=1, source_target_pairs={{4,6},{5,7},{12,14},{13,15},{20,22},{21,23},{28,30},{29,31}} | collective-permute-start | bytes 6291464 | tf_op jit(solution)/shard_map/ppermute | solution.py:57
  255.0 45.1 %collective-permute-start.97 = (bf16[4096,256]{1,0:T(8,128)(2,1)}, bf16[4096,256]{1,0:T(8,128)(2,1)}, u32[]{:S(2)}, u32[]{:S(2)}) collective-permute-start(bf16[4096,256]{1,0:T(8,128)(2,1)} %collective-permute-done.96), channel_id=1, source_target_pairs={{2,0},{3,1},{10,8},{11,9},{18,16},{19,17},{26,24},{27,25}} | collective-permute-start | bytes 6291464 | tf_op jit(solution)/shard_map/ppermute | solution.py:62
  259.8 35.3 %collective-permute-start.102 = (bf16[2048,256]{1,0:T(8,128)(2,1)}, bf16[2048,256]{1,0:T(8,128)(2,1)}, u32[]{:S(2)}, u32[]{:S(2)}) collective-permute-start(bf16[2048,256]{1,0:T(8,128)(2,1)} %get-tuple-element.219), channel_id=1, source_target_pairs={{0,1},{1,0},{2,3},{3,2},{4,5},{5,4},{6,7},{7,6},{8,9},{9,8},{10,11... | collective-permute-start | bytes 3145736 | tf_op jit(solution)/shard_map/ppermute | solution.py:39
  278.0 17.1 %copy-start.7 = (bf16[2048,256]{1,0:T(8,128)(2,1)S(1)}, bf16[2048,256]{1,0:T(8,128)(2,1)}, u32[]{:S(2)}) copy-start(bf16[2048,256]{1,0:T(8,128)(2,1)} %get-tuple-element.220) | copy-start | bytes 3145732
  278.0 17.1 %copy-start.8 = (bf16[2048,256]{1,0:T(8,128)(2,1)S(1)}, bf16[2048,256]{1,0:T(8,128)(2,1)}, u32[]{:S(2)}) copy-start(bf16[2048,256]{1,0:T(8,128)(2,1)} %get-tuple-element.221) | copy-start | bytes 3145732
  295.1 9.5 %slice-start = ((s8[8388608]{0:T(1024)(128)(4,1)}), s8[4194304]{0:T(1024)(128)(4,1)S(1)}, s32[]{:S(2)}) async-start(s8[8388608]{0:T(1024)(128)(4,1)} %bitcast.73), calls=%async_computation | async-start | bytes 8388608
  296.6 7.9 %slice-start.1 = ((s8[8388608]{0:T(1024)(128)(4,1)}), s8[4194304]{0:T(1024)(128)(4,1)S(1)}, s32[]{:S(2)}) async-start(s8[8388608]{0:T(1024)(128)(4,1)} %bitcast.73), calls=%async_computation.1 | async-start | bytes 8388608
  304.0 57.1 %collective-permute-start.98 = (bf16[4096,256]{1,0:T(8,128)(2,1)S(1)}, bf16[4096,256]{1,0:T(8,128)(2,1)S(1)}, u32[]{:S(2)}, u32[]{:S(2)}) collective-permute-start(bf16[4096,256]{1,0:T(8,128)(2,1)S(1)} %get-tuple-element.228), channel_id=1, source_target_pairs={{0,1},{1,0},{2,3},{3,2},{4,5},{5,4},{6,7},{7,6},{8,9},{9,8},{10,11... | collective-permute-start | bytes 6291464 | tf_op jit(solution)/shard_map/ppermute | solution.py:39
  338.2 19.1 %collective-permute-start.114 = (bf16[4,256,256]{2,1,0:T(8,128)(2,1)S(1)}, bf16[4,256,256]{2,1,0:T(8,128)(2,1)S(1)}, u32[]{:S(2)}, u32[]{:S(2)}) collective-permute-start(bf16[4,256,256]{2,1,0:T(8,128)(2,1)S(1)} %fusion.7), channel_id=1, source_target_pairs={{0,1},{1,0},{2,3},{3,2},{4,5},{5,4},{6,7},{7,6},{8,9},{9,8},{10,11... | collective-permute-start | bytes 1572872 | tf_op jit(solution)/shard_map/ppermute | solution.py:39
  357.4 6.9 %collective-permute-start.115 = (bf16[256,256]{1,0:T(8,128)(2,1)S(1)}, bf16[256,256]{1,0:T(8,128)(2,1)S(1)}, u32[]{:S(2)}, u32[]{:S(2)}) collective-permute-start(bf16[256,256]{1,0:T(8,128)(2,1)S(1)} %get-tuple-element.251), channel_id=1, source_target_pairs={{0,24},{8,16},{16,8},{24,0},{1,25},{9,17},{17,9},{25,1},{2,26},{10... | collective-permute-start | bytes 393224 | tf_op jit(solution)/shard_map/ppermute | solution.py:39
  359.1 8.5 %collective-permute-start.116 = (bf16[256,256]{1,0:T(8,128)(2,1)S(1)}, bf16[256,256]{1,0:T(8,128)(2,1)S(1)}, u32[]{:S(2)}, u32[]{:S(2)}) collective-permute-start(bf16[256,256]{1,0:T(8,128)(2,1)S(1)} %get-tuple-element.250), channel_id=1, source_target_pairs={{0,16},{8,24},{16,0},{24,8},{1,17},{9,25},{17,1},{25,9},{2,18},{10... | collective-permute-start | bytes 393224 | tf_op jit(solution)/shard_map/ppermute | solution.py:39
  361.0 6.6 %collective-permute-start.117 = (bf16[256,256]{1,0:T(8,128)(2,1)S(1)}, bf16[256,256]{1,0:T(8,128)(2,1)S(1)}, u32[]{:S(2)}, u32[]{:S(2)}) collective-permute-start(bf16[256,256]{1,0:T(8,128)(2,1)S(1)} %get-tuple-element.249), channel_id=1, source_target_pairs={{0,8},{8,0},{16,24},{24,16},{1,9},{9,1},{17,25},{25,17},{2,10},{10... | collective-permute-start | bytes 393224 | tf_op jit(solution)/shard_map/ppermute | solution.py:39
